TPU v7x, 32 devices: a whole 2x2x4 slice. The times are simulated.
32 devices in a mesh: seq: 8 (over z, y), tp: 4 (over x, core).
Axes of the slice: x: 2, y: 2, z: 4, core: 2. Of those that a mesh axis runs over, the one named last changes fastest.
Arguments:
- normed_input: bfloat16 [4096, 5376], P('seq', 'tp'), may hold values from -6 to 6
- query: bfloat16 [4096, 4096], P('seq', 'tp'), may hold values from -220 to 220, as said below
- key: bfloat16 [4096, 2048], P('seq', 'tp'), may hold values from -7 to 7
- value: bfloat16 [4096, 2048], P('seq', 'tp'), may hold values from -6 to 6
- adapter_down_maps: bfloat16 [64, 16, 5376], P(None, None, 'tp'), may hold values from -0.078125 to 0.078125
- adapter_up_maps: bfloat16 [64, 16, 2048], P(None, None, 'tp'), may hold values from -1.5 to 1.5
- block_adapter_choice: int32 [2], replicated, may hold values from 0 to 63
Outputs:
- attended: bfloat16 [4096, 4096], P('seq', 'tp')
Inputs may be any that keep to these rules, and one draw needn't show every extreme that they name: `query`: queries; some may be aligned with nearby keys.
All inputs are finite; a program needn't handle non-finite values.
Results may differ from a plain program's by a relative error of at most 0.014.
Values may be sent and summed in bfloat16 or wider, within the bound.
No kernel may reach another device: no remote copies, remote signals or barrier semaphores. Data moves between devices by JAX's collectives and lax.ppermute only.
A program may use at most 128 MiB of HBM per device.

v0:
```python
import functools

import jax
import jax.numpy as jnp
from jax import lax
from jax.experimental import pallas as pl
from jax.experimental.pallas import tpu as pltpu
from jax.sharding import PartitionSpec as P

HEAD_WIDTH = 128
WINDOW = 1024
SEG_LEN = 2048
SCALE = 168.0 ** (-0.5)
LOG2_E = 1.4426950408889634
EXPONENT = SCALE * LOG2_E
MASKED = -1e30
TILE = 256
HALF = 128
ONES = 16
PAIR = 2
PIECE = 256


def params(steps, mib):
    return pltpu.CompilerParams(
        vmem_limit_bytes=mib * 1024 * 1024, dimension_semantics=("arbitrary",) * steps
    )


def dot(left, right, left_dim, right_dim):
    return lax.dot_general(
        left, right, (((left_dim,), (right_dim,)), ((), ())), preferred_element_type=jnp.float32
    )


def in_hbm(array):
    return pltpu.with_memory_space_constraint(array, pltpu.HBM)


def adapter_of(choice, tok):
    return choice[lax.div(lax.axis_index("seq") * tok, SEG_LEN)]


def first_half_kernel(key, out, sem):
    copy = pltpu.make_async_copy(key.at[pl.ds(0, out.shape[0])], out, sem)
    copy.start()
    copy.wait()


def first_half(key):
    rows, columns = key.shape
    return pl.pallas_call(
        first_half_kernel,
        in_specs=[pl.BlockSpec(memory_space=pltpu.HBM)],
        out_specs=pl.BlockSpec(memory_space=pltpu.VMEM),
        out_shape=jax.ShapeDtypeStruct((rows // 2, columns), key.dtype),
        scratch_shapes=[pltpu.SemaphoreType.DMA],
        compiler_params=pltpu.CompilerParams(vmem_limit_bytes=8 * 1024 * 1024),
        name="first_half",
    )(in_hbm(key))


def latent_kernel(
    pieces, choice, input_t, down, up, key, out, up_out, key_out, ids, rows, map_rows, sems
):
    half = key_out.shape[0]
    ids_copy = pltpu.make_async_copy(choice, ids, sems.at[0])
    ids_copy.start()
    copies = []
    for n, (first, last) in enumerate(pieces):
        part = pl.ds(first, last - first)
        copies.append(pltpu.make_async_copy(input_t.at[part], rows.at[part], sems.at[n + 4]))
        copies[-1].start()
    key_copy = pltpu.make_async_copy(key.at[pl.ds(half, half)], key_out, sems.at[1])
    key_copy.start()
    ids_copy.wait()
    chosen = adapter_of(ids, out.shape[1])
    down_copy = pltpu.make_async_copy(down.at[chosen], map_rows, sems.at[2])
    up_copy = pltpu.make_async_copy(up.at[chosen], up_out, sems.at[3])
    down_copy.start()
    up_copy.start()
    down_copy.wait()
    total = None
    for (first, last), copy in zip(pieces, copies):
        copy.wait()
        product = dot(map_rows[:, first:last], rows[first:last, :], 1, 0)
        total = product if total is None else total + product
    out[...] = total
    up_copy.wait()
    key_copy.wait()


def latent_share(choice, input_t, down_maps, up_maps, key):
    features, tok = input_t.shape
    rank, columns = up_maps.shape[1:]
    pieces = [(first, min(first + PIECE, features)) for first in range(0, features, PIECE)]
    return pl.pallas_call(
        functools.partial(latent_kernel, pieces),
        in_specs=[pl.BlockSpec(memory_space=pltpu.HBM)] * 5,
        out_specs=[pl.BlockSpec(memory_space=pltpu.VMEM)] * 3,
        out_shape=[
            jax.ShapeDtypeStruct((rank, tok), jnp.float32),
            jax.ShapeDtypeStruct((rank, columns), up_maps.dtype),
            jax.ShapeDtypeStruct((tok // 2, columns), key.dtype),
        ],
        scratch_shapes=[
            pltpu.SMEM(choice.shape, choice.dtype),
            pltpu.VMEM((features, tok), input_t.dtype),
            pltpu.VMEM((rank, features), down_maps.dtype),
            pltpu.SemaphoreType.DMA((len(pieces) + 4,)),
        ],
        compiler_params=pltpu.CompilerParams(vmem_limit_bytes=8 * 1024 * 1024),
        name="latent_share",
    )(*(in_hbm(array) for array in (choice, input_t, down_maps, up_maps, key)))


def adapt_kernel(mine, theirs, up, value, *outs):
    latent = (mine[...] + theirs[...]).astype(jnp.bfloat16)
    update = dot(latent, up[...], 0, 0)
    total = (value[...].astype(jnp.float32) + update).astype(jnp.bfloat16)
    for n, out in enumerate(outs):
        width = out.shape[1]
        out[...] = total[:, n * width : (n + 1) * width]


def adapt(mine, theirs, up, value):
    tok, columns = value.shape
    width = PAIR * HEAD_WIDTH
    return pl.pallas_call(
        adapt_kernel,
        out_shape=[jax.ShapeDtypeStruct((tok, width), jnp.bfloat16)] * (columns // width),
        compiler_params=pltpu.CompilerParams(vmem_limit_bytes=8 * 1024 * 1024),
        name="adapt_values",
    )(mine, theirs, up, value)


def weights_of(scores, top):
    return jnp.exp2(((scores - top) * EXPONENT).astype(jnp.bfloat16))


def tree(operation, items):
    items = list(items)
    while len(items) > 1:
        items = [
            operation(items[n], items[n + 1]) if n + 1 < len(items) else items[n]
            for n in range(0, len(items), 2)
        ]
    return items[0]


def top_of(scores):
    pieces = [s[n : n + 32] for s in scores for n in range(0, s.shape[0], 32)]
    pieces = tree(jnp.maximum, pieces)
    pieces = tree(jnp.maximum, [pieces[n : n + 8] for n in range(0, 32, 8)])
    return jnp.max(pieces, axis=0, keepdims=True)


def values_and_ones(v, columns):
    turned = v[:, columns].T
    return jnp.concatenate([turned, jnp.ones((ONES, v.shape[0]), jnp.bfloat16)], axis=0)


def tile(halves, j, columns):
    rows = halves[0].shape[0]
    first = j * TILE % rows
    return halves[j * TILE // rows][first : first + TILE, columns]


def head_rows(h):
    return slice(h * (HEAD_WIDTH + ONES), (h + 1) * (HEAD_WIDTH + ONES))


def head_columns(h):
    return slice(h * HEAD_WIDTH, (h + 1) * HEAD_WIDTH)


def in_steps(units, stages):
    held = [None] * len(units)
    for step in range(len(units) + len(stages) - 1):
        for n, stage in enumerate(stages):
            if 0 <= step - n < len(units):
                held[step - n] = stage(units[step - n], held[step - n])


def units_of(group, tok, kv_heads):
    return [
        (h, i)
        for g in kv_heads
        for i in range(tok // TILE)
        for h in range(g * group, (g + 1) * group)
    ]


def near_far_kernel(group, *refs):
    place = lax.axis_index("seq")

    @pl.when(place >= 2)
    def _():
        near_far_steps(group, True, *refs)

    @pl.when(place < 2)
    def _():
        near_far_steps(group, False, *refs)


def near_far_steps(
    group, far_there, q, k_1, k_2, v_a, v_b, k_far_1, k_far_2, out, weights_far, tops
):
    k, v, k_far = (k_1, k_2), (v_a, v_b), (k_far_1, k_far_2)
    tok = q.shape[0]
    kv_heads = range(k_1.shape[1] // HEAD_WIDTH)
    causal = lax.broadcasted_iota(jnp.int32, (HALF, HALF), 0) <= lax.broadcasted_iota(
        jnp.int32, (HALF, HALF), 1
    )
    v_t = [values_and_ones(v[g // PAIR], head_columns(g % PAIR)) for g in kv_heads]
    nothing = jnp.zeros((HALF, HALF), jnp.bfloat16)
    tiles = tok // TILE
    blocks = [slice(i * TILE, (i + 1) * TILE) for i in range(tiles)]

    def score(unit, _):
        h, i = unit
        qh = q[blocks[i], head_columns(h)]
        columns = head_columns(h // group)
        near = [dot(tile(k, j, columns), qh, 1, 1) for j in range(i + 1)]
        far = []
        if far_there:
            far = [dot(tile(k_far, j, columns), qh, 1, 1) for j in range(i, tiles)]
        return near, far

    def weigh(unit, scores):
        h, i = unit
        near, far = scores
        near_columns, far_columns = [], []
        for half in range(2):
            a = slice(half * HALF, (half + 1) * HALF)
            near_edge = near[i][: (half + 1) * HALF, a]
            near_pieces = [s[:, a] for s in near[:i]]
            if half == 1:
                near_pieces.append(near_edge[:HALF])
            near_pieces.append(jnp.where(causal, near_edge[half * HALF :], MASKED))
            far_pieces = []
            if far_there:
                far_edge = far[0][half * HALF :, a]
                far_pieces.append(jnp.where(causal, MASKED, far_edge[:HALF]))
                if half == 0:
                    far_pieces.append(far_edge[HALF:])
                far_pieces += [s[:, a] for s in far[1:]]
            top = top_of(near_pieces + far_pieces)
            near_weights = [weights_of(s, top) for s in near_pieces]
            if half == 0:
                near_weights.append(nothing)
            near_columns.append(jnp.concatenate(near_weights, axis=0))
            if far_there:
                far_weights = [weights_of(s, top) for s in far_pieces]
                if half == 1:
                    far_weights.insert(0, nothing)
                far_columns.append(jnp.concatenate(far_weights, axis=0))
            queries = slice(i * TILE + half * HALF, i * TILE + (half + 1) * HALF)
            tops[h : h + 1, queries] = top
        if far_there:
            weights_far[h, i * TILE :, blocks[i]] = jnp.concatenate(far_columns, axis=1)
        return jnp.concatenate(near_columns, axis=1)

    def multiply(unit, weights):
        h, i = unit
        out[head_rows(h), blocks[i]] = dot(v_t[h // group][:, : (i + 1) * TILE], weights, 1, 0)

    in_steps(units_of(group, tok, kv_heads), [score, weigh, multiply])


def middle_kernel(group, *refs):
    place = lax.axis_index("seq")

    @pl.when(place >= 2)
    def _():
        middle_steps(group, True, *refs)

    @pl.when(place == 1)
    def _():
        middle_steps(group, False, *refs)

    @pl.when(place == 0)
    def _():
        q, own, k, out, stage, sems = refs[0], refs[1], refs[4], refs[10], refs[11], refs[12]
        kv_heads = range(k.shape[1] // HEAD_WIDTH)
        write_steps(
            group, kv_heads, q.shape[0], lambda h, b: own[head_rows(h), b], out, stage, sems
        )


def middle_steps(
    group, far_there, q, own, weights_far, tops, k_1, k_2, v_a, v_b, rest, weights, *_
):
    k, v_far = (k_1, k_2), (v_a, v_b)
    tok = q.shape[0]
    kv_heads = range(k_1.shape[1] // HEAD_WIDTH)
    v_t = []
    if far_there:
        v_t = [values_and_ones(v_far[g // PAIR], head_columns(g % PAIR)) for g in kv_heads]
    tiles = tok // TILE
    blocks = [slice(i * TILE, (i + 1) * TILE) for i in range(tiles)]

    def score(unit, _):
        h, i = unit
        qh = q[blocks[i], head_columns(h)]
        return [dot(tile(k, j, head_columns(h // group)), qh, 1, 1) for j in range(tiles)]

    def weigh(unit, scores):
        h, i = unit
        before = tops[h : h + 1, blocks[i]]
        top = jnp.maximum(before, top_of(scores))
        for j, s in enumerate(scores):
            weights[h, blocks[j], blocks[i]] = weights_of(s, top)
        return jnp.exp2((before - top) * EXPONENT)

    def multiply(unit, less):
        h, i = unit
        total = own[head_rows(h), blocks[i]]
        if far_there:
            total += dot(v_t[h // group][:, i * TILE :], weights_far[h, i * TILE :, blocks[i]], 1, 0)
        rest[head_rows(h), blocks[i]] = total * less

    in_steps(units_of(group, tok, kv_heads), [score, weigh, multiply])


def write_steps(group, kv_heads, tok, total_of, out, stage, sems):
    copies = []
    for h, i in units_of(group, tok, kv_heads):
        b = slice(i * TILE, (i + 1) * TILE)
        total = total_of(h, b)
        normal = total[:HEAD_WIDTH] * (1.0 / total[HEAD_WIDTH : HEAD_WIDTH + 1])
        stage[b, head_columns(h)] = normal.astype(jnp.bfloat16).T
        if h % group == group - 1:
            width = group * HEAD_WIDTH
            part = (pl.ds(i * TILE, TILE), pl.ds((h + 1) * HEAD_WIDTH - width, width))
            copies.append(
                pltpu.make_async_copy(stage.at[part], out.at[part], sems.at[len(copies)])
            )
            copies[-1].start()
    for copy in copies:
        copy.wait()


def finish_kernel(group, rest, weights, v, _, out, stage, sems, part):
    tok = weights.shape[1]
    kv_heads = range(part * PAIR, (part + 1) * PAIR)

    @pl.when(lax.axis_index("seq") >= 1)
    def _():
        v_t = [values_and_ones(v, head_columns(g % PAIR)) for g in kv_heads]
        units = units_of(group, tok, kv_heads)
        held = []

        def total_of(h, b):
            at = units.index((h, b.start // TILE))
            for m, i in units[len(held) : at + 2]:
                c = slice(i * TILE, (i + 1) * TILE)
                held.append(dot(v_t[m // group - part * PAIR], weights[m, :, c], 1, 0))
            return rest[head_rows(h), b] + held[at]

        write_steps(group, kv_heads, tok, total_of, out, stage, sems)


def by_heads(
    kernel, name, query_shape, columns, arrays, out_kinds, into=None
):
    tok, width = query_shape
    heads = width // HEAD_WIDTH
    shapes = dict(
        rest=((heads * (HEAD_WIDTH + ONES), tok), jnp.float32),
        weights=((heads, tok, tok), jnp.bfloat16),
        stat=((heads, tok), jnp.float32),
        output=((tok, width), jnp.bfloat16),
    )
    in_vmem, anywhere = pl.BlockSpec(memory_space=pltpu.VMEM), pl.BlockSpec(memory_space=pl.ANY)
    in_specs = [in_vmem] * len(arrays)
    aliases, scratch = {}, []
    if into is not None:
        aliases = {len(arrays): out_kinds.index("output")}
        arrays.append(into)
        in_specs.append(anywhere)
    if "output" in out_kinds:
        copies = columns // HEAD_WIDTH * (tok // TILE)
        scratch = [
            pltpu.VMEM((tok, width), jnp.bfloat16),
            pltpu.SemaphoreType.DMA((copies,)),
        ]
    return pl.pallas_call(
        functools.partial(kernel, width // columns),
        in_specs=in_specs,
        out_specs=[anywhere if kind == "output" else in_vmem for kind in out_kinds],
        scratch_shapes=scratch,
        out_shape=[jax.ShapeDtypeStruct(*shapes[kind]) for kind in out_kinds],
        input_output_aliases=aliases,
        compiler_params=pltpu.CompilerParams(vmem_limit_bytes=24 * 1024 * 1024),
        name=name,
    )(*arrays)


def shifted(array, steps):
    count = lax.axis_size("seq")
    return lax.ppermute(array, "seq", [(source, source + steps) for source in range(count - steps)])


def exchanged(array, axis, bit):
    count = lax.axis_size(axis)
    return lax.ppermute(array, axis, [(source, source ^ bit) for source in range(count)])


def on_device(
    normed_input, query, key, value, adapter_down_maps, adapter_up_maps, block_adapter_choice
):
    tok = query.shape[0]
    assert 2 * tok == WINDOW and SEG_LEN % tok == 0
    where = lax.axis_index("seq")
    choice = block_adapter_choice

    even = where % 2 == 0
    barrier = lax.optimization_barrier
    call = functools.partial(by_heads, query_shape=query.shape, columns=key.shape[1])

    def from_one_back(own, far):
        return exchanged(jnp.where(even, own, far), "seq", 1)

    key_1 = first_half(key)
    key_far_1 = shifted(key_1, 2)
    latent, up, key_2 = latent_share(
        choice, normed_input.T, adapter_down_maps, adapter_up_maps, key
    )
    key_far_2 = shifted(key_2, 2)
    bit = lax.axis_size("tp") // 2
    while bit > 1:
        latent = latent + exchanged(latent, "tp", bit)
        bit //= 2
    key_1, latent = barrier((key_1, latent))
    theirs = exchanged(latent, "tp", bit)
    key_mid_1 = from_one_back(key_1, key_far_1)
    values = adapt(latent, theirs, up, value)
    value_far = [shifted(part, 2) for part in values]
    key_2, values = barrier((key_2, values))
    key_mid_2 = from_one_back(key_2, key_far_2)
    values, key_mid_1 = barrier((values, key_mid_1))
    own, weights_far, tops = call(
        near_far_kernel,
        "near_far",
        arrays=[query, key_1, key_2, *values, key_far_1, key_far_2],
        out_kinds=["rest", "weights", "stat"],
    )
    values, own = barrier((values, own))
    value_mid = [from_one_back(mine, theirs) for mine, theirs in zip(values, value_far)]
    rest, weights_mid, done = call(
        middle_kernel,
        "middle",
        arrays=[query, own, weights_far, tops, key_mid_1, key_mid_2, *value_far],
        out_kinds=["rest", "weights", "output"],
    )
    for n, part in enumerate(value_mid):
        [done] = call(
            functools.partial(finish_kernel, part=n),
            "finish",
            arrays=[rest, weights_mid, part],
            out_kinds=["output"],
            into=done,
        )
    return done


def solution(mesh):
    placed = (
        P("seq", "tp"),
        P("seq", "tp"),
        P("seq", "tp"),
        P("seq", "tp"),
        P(None, None, "tp"),
        P(None, None, "tp"),
        P(),
    )
    return jax.shard_map(
        on_device, mesh=mesh, in_specs=placed, out_specs=P("seq", "tp"), check_vma=False
    )
```

profile of v0, /device:TPU:0, one launch (start us, length us, event | category | flops | bytes accessed | tf_op | source)
XLA Modules:
  0.0 40.6 jit_solution(2427407086462580067)
XLA Ops:
  0.0 1.0 %first_half.1.refs_1_ = bf16[256,512]{1,0:T(8,128)(2,1)S(1)} custom-call(bf16[512,512]{1,0:T(8,128)(2,1)} %key.3), custom_call_target="tpu_custom_call" | custom-call | tf_op jit(solution)/shard_map/first_half/pallas_call | solution.py:52
  1.0 4.9 %collective-permute-start.2 = (bf16[256,512]{1,0:T(8,128)(2,1)S(1)}, bf16[256,512]{1,0:T(8,128)(2,1)S(1)}, u32[]{:S(2)}, u32[]{:S(2)}) collective-permute-start(bf16[256,512]{1,0:T(8,128)(2,1)S(1)} %first_half.1.refs_1_), channel_id=1, source_target_pairs={{0,8},{4,12},{8,16},{12,20},{16,24},{20,28},{1,9},{5,13},{9,17},{1... | collective-permute-start | bytes 786440 | tf_op jit(solution)/shard_map/ppermute | solution.py:402
  5.9 0.0 copy-start.1
  5.9 0.0 copy-start
  5.9 2.3 %latent_share.1 = (f32[16,512]{1,0:T(8,128)S(1)}, bf16[16,512]{1,0:T(8,128)(2,1)S(1)}, bf16[256,512]{1,0:T(8,128)(2,1)S(1)}) custom-call(s32[2]{0:T(128)} %choice.1, bf16[1344,512]{1,0:T(8,128)(2,1)} %bitcast.1, bf16[64,16,1344]{2,1,0:T(8,128)(2,1)} %down.1, bf16[64,16,512]{2,1,0:T(8,128)(2,1)} %up.1, bf16[512,512]{1,0:T(8,128)(2,1)} %key.3), custom_call_target="tpu_custom_call" | custom-call | tf_op jit(solution)/shard_map/latent_share/pallas_call | solution.py:97
  8.2 1.6 %collective-permute-start = (f32[16,512]{1,0:T(8,128)S(1)}, f32[16,512]{1,0:T(8,128)S(1)}, u32[]{:S(2)}, u32[]{:S(2)}) collective-permute-start(f32[16,512]{1,0:T(8,128)S(1)} %get-tuple-element.28), channel_id=1, source_target_pairs={{0,2},{1,3},{2,0},{3,1},{4,6},{5,7},{6,4},{7,5},{8,10},{9,11},{10,... | collective-permute-start | bytes 98312 | tf_op jit(solution)/shard_map/ppermute | solution.py:407
  9.8 3.5 %collective-permute-start.4 = (bf16[256,512]{1,0:T(8,128)(2,1)S(1)}, bf16[256,512]{1,0:T(8,128)(2,1)S(1)}, u32[]{:S(2)}, u32[]{:S(2)}) collective-permute-start(bf16[256,512]{1,0:T(8,128)(2,1)S(1)} %get-tuple-element.38.refs_2_), channel_id=1, source_target_pairs={{0,8},{4,12},{8,16},{12,20},{16,24},{20,28},{1,9},{5,13},{9,17},{1... | collective-permute-start | bytes 786440 | tf_op jit(solution)/shard_map/ppermute | solution.py:402
  13.3 0.0 collective-permute-done
  13.3 0.1 collective-permute-start.1
  13.4 1.6 %collective-permute-start.3 = (bf16[256,512]{1,0:T(8,128)(2,1)S(1)}, bf16[256,512]{1,0:T(8,128)(2,1)S(1)}, u32[]{:S(2)}, u32[]{:S(2)}) collective-permute-start(bf16[256,512]{1,0:T(8,128)(2,1)S(1)} %broadcast_select_fusion.3), channel_id=1, source_target_pairs={{0,4},{4,0},{8,12},{12,8},{16,20},{20,16},{24,28},{28,24},{1,5},{5... | collective-permute-start | bytes 786440 | tf_op jit(solution)/shard_map/ppermute | solution.py:407
  15.0 0.3 adapt_values.1
  15.3 3.5 %collective-permute-start.6 = (bf16[512,256]{1,0:T(8,128)(2,1)S(1)}, bf16[512,256]{1,0:T(8,128)(2,1)S(1)}, u32[]{:S(2)}, u32[]{:S(2)}) collective-permute-start(bf16[512,256]{1,0:T(8,128)(2,1)S(1)} %get-tuple-element.47.refs_3_), channel_id=1, source_target_pairs={{0,8},{4,12},{8,16},{12,20},{16,24},{20,28},{1,9},{5,13},{9,17},{1... | collective-permute-start | bytes 786440 | tf_op jit(solution)/shard_map/ppermute | solution.py:402
  18.8 2.5 %collective-permute-start.7 = (bf16[512,256]{1,0:T(8,128)(2,1)S(1)}, bf16[512,256]{1,0:T(8,128)(2,1)S(1)}, u32[]{:S(2)}, u32[]{:S(2)}) collective-permute-start(bf16[512,256]{1,0:T(8,128)(2,1)S(1)} %get-tuple-element.46.refs_4_), channel_id=1, source_target_pairs={{0,8},{4,12},{8,16},{12,20},{16,24},{20,28},{1,9},{5,13},{9,17},{1... | collective-permute-start | bytes 786440 | tf_op jit(solution)/shard_map/ppermute | solution.py:402
  21.4 1.0 %collective-permute-start.5 = (bf16[256,512]{1,0:T(8,128)(2,1)S(1)}, bf16[256,512]{1,0:T(8,128)(2,1)S(1)}, u32[]{:S(2)}, u32[]{:S(2)}) collective-permute-start(bf16[256,512]{1,0:T(8,128)(2,1)S(1)} %broadcast_select_fusion.2), channel_id=1, source_target_pairs={{0,4},{4,0},{8,12},{12,8},{16,20},{20,16},{24,28},{28,24},{1,5},{5... | collective-permute-start | bytes 786440 | tf_op jit(solution)/shard_map/ppermute | solution.py:407
  22.4 2.2 %near_far.1 = (f32[1152,512]{1,0:T(8,128)S(1)}, bf16[8,512,512]{2,1,0:T(8,128)(2,1)S(1)}, f32[8,512]{1,0:T(8,128)S(1)}) custom-call(bf16[512,1024]{1,0:T(8,128)(2,1)S(1)} %copy-done, bf16[256,512]{1,0:T(8,128)(2,1)S(1)} %first_half.1.refs_1_, bf16[256,512]{1,0:T(8,128)(2,1)S(1)} %get-tuple-element.38.refs_2_, ...), custom_call_target="tpu_custom_call" | custom-call | tf_op jit(solution)/shard_map/near_far/pallas_call | solution.py:388
  24.6 0.9 %collective-permute-done.6.refs_6_ = bf16[512,256]{1,0:T(8,128)(2,1)S(1)} collective-permute-done((bf16[512,256]{1,0:T(8,128)(2,1)S(1)}, bf16[512,256]{1,0:T(8,128)(2,1)S(1)}, u32[]{:S(2)}, u32[]{:S(2)}) %collective-permute-start.6) | collective-permute-done | bytes 262176 | tf_op jit(solution)/shard_map/ppermute | solution.py:402
  25.5 1.1 %collective-permute-start.9 = (bf16[512,256]{1,0:T(8,128)(2,1)S(1)}, bf16[512,256]{1,0:T(8,128)(2,1)S(1)}, u32[]{:S(2)}, u32[]{:S(2)}) collective-permute-start(bf16[512,256]{1,0:T(8,128)(2,1)S(1)} %broadcast_select_fusion), channel_id=1, source_target_pairs={{0,4},{4,0},{8,12},{12,8},{16,20},{20,16},{24,28},{28,24},{1,5},{5... | collective-permute-start | bytes 786440 | tf_op jit(solution)/shard_map/ppermute | solution.py:407
  26.6 3.7 %collective-permute-done.7.refs_7_ = bf16[512,256]{1,0:T(8,128)(2,1)S(1)} collective-permute-done((bf16[512,256]{1,0:T(8,128)(2,1)S(1)}, bf16[512,256]{1,0:T(8,128)(2,1)S(1)}, u32[]{:S(2)}, u32[]{:S(2)}) %collective-permute-start.7) | collective-permute-done | bytes 262176 | tf_op jit(solution)/shard_map/ppermute | solution.py:402
  30.4 1.1 %collective-permute-start.8 = (bf16[512,256]{1,0:T(8,128)(2,1)S(1)}, bf16[512,256]{1,0:T(8,128)(2,1)S(1)}, u32[]{:S(2)}, u32[]{:S(2)}) collective-permute-start(bf16[512,256]{1,0:T(8,128)(2,1)S(1)} %broadcast_select_fusion.1), channel_id=1, source_target_pairs={{0,4},{4,0},{8,12},{12,8},{16,20},{20,16},{24,28},{28,24},{1,5},{5... | collective-permute-start | bytes 786440 | tf_op jit(solution)/shard_map/ppermute | solution.py:407
  31.5 1.1 %middle.1 = (f32[1152,512]{1,0:T(8,128)S(1)}, bf16[8,512,512]{2,1,0:T(8,128)(2,1)S(1)}, bf16[512,1024]{1,0:T(8,128)(2,1)}) custom-call(bf16[512,1024]{1,0:T(8,128)(2,1)S(1)} %copy-done, f32[1152,512]{1,0:T(8,128)S(1)} %get-tuple-element.40.refs_1_, bf16[8,512,512]{2,1,0:T(8,128)(2,1)S(1)} %get-tuple-element.41.refs_2_, ...), custom_call_target="tpu_custom_call" | custom-call | tf_op jit(solution)/shard_map/middle/pallas_call | solution.py:388
  32.6 3.7 %collective-permute-done.9.v = bf16[512,256]{1,0:T(8,128)(2,1)S(1)} collective-permute-done((bf16[512,256]{1,0:T(8,128)(2,1)S(1)}, bf16[512,256]{1,0:T(8,128)(2,1)S(1)}, u32[]{:S(2)}, u32[]{:S(2)}) %collective-permute-start.9) | collective-permute-done | bytes 262176 | tf_op jit(solution)/shard_map/ppermute | solution.py:407
  36.3 0.1 finish.2._
  36.4 4.0 %collective-permute-done.8.v = bf16[512,256]{1,0:T(8,128)(2,1)S(1)} collective-permute-done((bf16[512,256]{1,0:T(8,128)(2,1)S(1)}, bf16[512,256]{1,0:T(8,128)(2,1)S(1)}, u32[]{:S(2)}, u32[]{:S(2)}) %collective-permute-start.8) | collective-permute-done | bytes 262176 | tf_op jit(solution)/shard_map/ppermute | solution.py:407
  40.4 0.1 finish.3
  (12 shorter events, 0.1 us)
Async XLA Ops:
  1.0 12.4 %collective-permute-start.2 = (bf16[256,512]{1,0:T(8,128)(2,1)S(1)}, bf16[256,512]{1,0:T(8,128)(2,1)S(1)}, u32[]{:S(2)}, u32[]{:S(2)}) collective-permute-start(bf16[256,512]{1,0:T(8,128)(2,1)S(1)} %first_half.1.refs_1_), channel_id=1, source_target_pairs={{0,8},{4,12},{8,16},{12,20},{16,24},{20,28},{1,9},{5,13},{9,17},{1... | collective-permute-start | bytes 786440 | tf_op jit(solution)/shard_map/ppermute | solution.py:402
  5.9 9.1 %copy-start.1 = (bf16[512,512]{1,0:T(8,128)(2,1)S(1)}, bf16[512,512]{1,0:T(8,128)(2,1)}, u32[]{:S(2)}) copy-start(bf16[512,512]{1,0:T(8,128)(2,1)} %value.1) | copy-start | bytes 1572868
  5.9 16.4 %copy-start = (bf16[512,1024]{1,0:T(8,128)(2,1)S(1)}, bf16[512,1024]{1,0:T(8,128)(2,1)}, u32[]{:S(2)}) copy-start(bf16[512,1024]{1,0:T(8,128)(2,1)} %refs_0_.3) | copy-start | bytes 3145732
  8.2 5.1 %collective-permute-start = (f32[16,512]{1,0:T(8,128)S(1)}, f32[16,512]{1,0:T(8,128)S(1)}, u32[]{:S(2)}, u32[]{:S(2)}) collective-permute-start(f32[16,512]{1,0:T(8,128)S(1)} %get-tuple-element.28), channel_id=1, source_target_pairs={{0,2},{1,3},{2,0},{3,1},{4,6},{5,7},{6,4},{7,5},{8,10},{9,11},{10,... | collective-permute-start | bytes 98312 | tf_op jit(solution)/shard_map/ppermute | solution.py:407
  9.8 11.5 %collective-permute-start.4 = (bf16[256,512]{1,0:T(8,128)(2,1)S(1)}, bf16[256,512]{1,0:T(8,128)(2,1)S(1)}, u32[]{:S(2)}, u32[]{:S(2)}) collective-permute-start(bf16[256,512]{1,0:T(8,128)(2,1)S(1)} %get-tuple-element.38.refs_2_), channel_id=1, source_target_pairs={{0,8},{4,12},{8,16},{12,20},{16,24},{20,28},{1,9},{5,13},{9,17},{1... | collective-permute-start | bytes 786440 | tf_op jit(solution)/shard_map/ppermute | solution.py:402
  13.3 1.7 %collective-permute-start.1 = (f32[16,512]{1,0:T(8,128)S(1)}, f32[16,512]{1,0:T(8,128)S(1)}, u32[]{:S(2)}, u32[]{:S(2)}) collective-permute-start(f32[16,512]{1,0:T(8,128)S(1)} %add.7.mine), channel_id=1, source_target_pairs={{0,1},{1,0},{2,3},{3,2},{4,5},{5,4},{6,7},{7,6},{8,9},{9,8},{10,11... | collective-permute-start | bytes 98312 | tf_op jit(solution)/shard_map/ppermute | solution.py:407
  13.4 8.9 %collective-permute-start.3 = (bf16[256,512]{1,0:T(8,128)(2,1)S(1)}, bf16[256,512]{1,0:T(8,128)(2,1)S(1)}, u32[]{:S(2)}, u32[]{:S(2)}) collective-permute-start(bf16[256,512]{1,0:T(8,128)(2,1)S(1)} %broadcast_select_fusion.3), channel_id=1, source_target_pairs={{0,4},{4,0},{8,12},{12,8},{16,20},{20,16},{24,28},{28,24},{1,5},{5... | collective-permute-start | bytes 786440 | tf_op jit(solution)/shard_map/ppermute | solution.py:407
  15.3 10.1 %collective-permute-start.6 = (bf16[512,256]{1,0:T(8,128)(2,1)S(1)}, bf16[512,256]{1,0:T(8,128)(2,1)S(1)}, u32[]{:S(2)}, u32[]{:S(2)}) collective-permute-start(bf16[512,256]{1,0:T(8,128)(2,1)S(1)} %get-tuple-element.47.refs_3_), channel_id=1, source_target_pairs={{0,8},{4,12},{8,16},{12,20},{16,24},{20,28},{1,9},{5,13},{9,17},{1... | collective-permute-start | bytes 786440 | tf_op jit(solution)/shard_map/ppermute | solution.py:402
  18.8 11.5 %collective-permute-start.7 = (bf16[512,256]{1,0:T(8,128)(2,1)S(1)}, bf16[512,256]{1,0:T(8,128)(2,1)S(1)}, u32[]{:S(2)}, u32[]{:S(2)}) collective-permute-start(bf16[512,256]{1,0:T(8,128)(2,1)S(1)} %get-tuple-element.46.refs_4_), channel_id=1, source_target_pairs={{0,8},{4,12},{8,16},{12,20},{16,24},{20,28},{1,9},{5,13},{9,17},{1... | collective-permute-start | bytes 786440 | tf_op jit(solution)/shard_map/ppermute | solution.py:402
  21.4 10.1 %collective-permute-start.5 = (bf16[256,512]{1,0:T(8,128)(2,1)S(1)}, bf16[256,512]{1,0:T(8,128)(2,1)S(1)}, u32[]{:S(2)}, u32[]{:S(2)}) collective-permute-start(bf16[256,512]{1,0:T(8,128)(2,1)S(1)} %broadcast_select_fusion.2), channel_id=1, source_target_pairs={{0,4},{4,0},{8,12},{12,8},{16,20},{20,16},{24,28},{28,24},{1,5},{5... | collective-permute-start | bytes 786440 | tf_op jit(solution)/shard_map/ppermute | solution.py:407
  25.5 10.8 %collective-permute-start.9 = (bf16[512,256]{1,0:T(8,128)(2,1)S(1)}, bf16[512,256]{1,0:T(8,128)(2,1)S(1)}, u32[]{:S(2)}, u32[]{:S(2)}) collective-permute-start(bf16[512,256]{1,0:T(8,128)(2,1)S(1)} %broadcast_select_fusion), channel_id=1, source_target_pairs={{0,4},{4,0},{8,12},{12,8},{16,20},{20,16},{24,28},{28,24},{1,5},{5... | collective-permute-start | bytes 786440 | tf_op jit(solution)/shard_map/ppermute | solution.py:407
  30.4 10.0 %collective-permute-start.8 = (bf16[512,256]{1,0:T(8,128)(2,1)S(1)}, bf16[512,256]{1,0:T(8,128)(2,1)S(1)}, u32[]{:S(2)}, u32[]{:S(2)}) collective-permute-start(bf16[512,256]{1,0:T(8,128)(2,1)S(1)} %broadcast_select_fusion.1), channel_id=1, source_target_pairs={{0,4},{4,0},{8,12},{12,8},{16,20},{20,16},{24,28},{28,24},{1,5},{5... | collective-permute-start | bytes 786440 | tf_op jit(solution)/shard_map/ppermute | solution.py:407
where the time goes:
time: 40.8 us; the launch traced here: 40.6 us
  starting transfers between devices  20.8 us (51%)
  waiting for transfers between devices  12.3 us (30%)
  Pallas kernels  7.03 us (17%)
    ppermute x4, starting transfers between devices, shifted(): lax.ppermute(array, 'seq', [(source, source + steps) for source in range(...  14.4 us
    ppermute x6, waiting for transfers between devices, exchanged(): lax.ppermute(array, axis, [(source, source ^ bit) for source in range(cou...  7.68 us
    ppermute x6, starting transfers between devices, exchanged(): lax.ppermute(array, axis, [(source, source ^ bit) for source in range(cou...  6.46 us
    ppermute x4, waiting for transfers between devices, shifted(): lax.ppermute(array, 'seq', [(source, source + steps) for source in range(...  4.59 us
    pallas_call x4, Pallas kernels, by_heads(): pl.pallas_call(functools.partial(kernel, width // columns), in_specs=in_s...  3.49 us
    pallas_call x1, Pallas kernels, latent_share(): pl.pallas_call(functools.partial(latent_kernel, pieces), in_specs=[pl.Blo...  2.26 us
    pallas_call x1, Pallas kernels, first_half(): pl.pallas_call(first_half_kernel, in_specs=[pl.BlockSpec(memory_space=plt...  0.96 us
  transfers between devices with their start and end apart: 10, of which 4 were waited for; matrix products, arithmetic and copies ran while one was open for 0% of the time, Pallas kernels for 15%

commit v1 on v0

--- a/solution.py
+++ b/solution.py
@@ -428,10 +428,10 @@
         choice, normed_input.T, adapter_down_maps, adapter_up_maps, key
     )
     key_far_2 = shifted(key_2, 2)
-    bit = lax.axis_size("tp") // 2
-    while bit > 1:
+    bit = 1
+    while 2 * bit < lax.axis_size("tp"):
         latent = latent + exchanged(latent, "tp", bit)
-        bit //= 2
+        bit *= 2
     key_1, latent = barrier((key_1, latent))
     theirs = exchanged(latent, "tp", bit)
     key_mid_1 = from_one_back(key_1, key_far_1)

time: 40.8 us -> 40.6 us (level)
  waiting for transfers between devices: 12.3 us -> 11.1 us
  starting transfers between devices: 20.8 us -> 21.8 us
    ppermute x6, starting transfers between devices: 6.46 us -> 7.96 us  [exchanged(): lax.ppermute(array, axis, [(source, source ^ bit) for source in range(cou...]
    ppermute x4, waiting for transfers between devices: 4.59 us -> 3.26 us  [shifted(): lax.ppermute(array, 'seq', [(source, source + steps) for source in range(...]
    ppermute x4, starting transfers between devices: 14.4 us -> 13.8 us  [shifted(): lax.ppermute(array, 'seq', [(source, source + steps) for source in range(...]
  transfers between devices with their start and end apart: 10 -> 10, of which waited for: 4 -> 5; matrix products, arithmetic and copies ran while one was open for 0% -> 0% of each run, Pallas kernels for 15% -> 15%
where the time goes in v1:
time: 40.6 us; the launch traced here: 40.4 us
  starting transfers between devices  21.8 us (54%)
  waiting for transfers between devices  11.1 us (27%)
  Pallas kernels  7.03 us (17%)
    ppermute x4, starting transfers between devices, shifted(): lax.ppermute(array, 'seq', [(source, source + steps) for source in range(...  13.8 us
    ppermute x6, starting transfers between devices, exchanged(): lax.ppermute(array, axis, [(source, source ^ bit) for source in range(cou...  7.96 us
    ppermute x6, waiting for transfers between devices, exchanged(): lax.ppermute(array, axis, [(source, source ^ bit) for source in range(cou...  7.87 us
    pallas_call x4, Pallas kernels, by_heads(): pl.pallas_call(functools.partial(kernel, width // columns), in_specs=in_s...  3.49 us
    ppermute x4, waiting for transfers between devices, shifted(): lax.ppermute(array, 'seq', [(source, source + steps) for source in range(...  3.26 us
    pallas_call x1, Pallas kernels, latent_share(): pl.pallas_call(functools.partial(latent_kernel, pieces), in_specs=[pl.Blo...  2.26 us
    pallas_call x1, Pallas kernels, first_half(): pl.pallas_call(first_half_kernel, in_specs=[pl.BlockSpec(memory_space=plt...  0.96 us
  transfers between devices with their start and end apart: 10, of which 5 were waited for; matrix products, arithmetic and copies ran while one was open for 0% of the time, Pallas kernels for 15%

profile of v1, /device:TPU:0, one launch (start us, length us, event | category | flops | bytes accessed | tf_op | source)
XLA Modules:
  0.0 40.4 jit_solution(17563196110772388491)
XLA Ops:
  0.0 1.0 %first_half.1.refs_1_ = bf16[256,512]{1,0:T(8,128)(2,1)S(1)} custom-call(bf16[512,512]{1,0:T(8,128)(2,1)} %key.3), custom_call_target="tpu_custom_call" | custom-call | tf_op jit(solution)/shard_map/first_half/pallas_call | solution.py:52
  1.0 4.9 %collective-permute-start.2 = (bf16[256,512]{1,0:T(8,128)(2,1)S(1)}, bf16[256,512]{1,0:T(8,128)(2,1)S(1)}, u32[]{:S(2)}, u32[]{:S(2)}) collective-permute-start(bf16[256,512]{1,0:T(8,128)(2,1)S(1)} %first_half.1.refs_1_), channel_id=1, source_target_pairs={{0,8},{4,12},{8,16},{12,20},{16,24},{20,28},{1,9},{5,13},{9,17},{1... | collective-permute-start | bytes 786440 | tf_op jit(solution)/shard_map/ppermute | solution.py:402
  5.9 0.0 copy-start.1
  5.9 0.0 copy-start
  5.9 2.3 %latent_share.1 = (f32[16,512]{1,0:T(8,128)S(1)}, bf16[16,512]{1,0:T(8,128)(2,1)S(1)}, bf16[256,512]{1,0:T(8,128)(2,1)S(1)}) custom-call(s32[2]{0:T(128)} %choice.1, bf16[1344,512]{1,0:T(8,128)(2,1)} %bitcast.1, bf16[64,16,1344]{2,1,0:T(8,128)(2,1)} %down.1, bf16[64,16,512]{2,1,0:T(8,128)(2,1)} %up.1, bf16[512,512]{1,0:T(8,128)(2,1)} %key.3), custom_call_target="tpu_custom_call" | custom-call | tf_op jit(solution)/shard_map/latent_share/pallas_call | solution.py:97
  8.2 0.1 collective-permute-start
  8.3 3.5 %collective-permute-start.4 = (bf16[256,512]{1,0:T(8,128)(2,1)S(1)}, bf16[256,512]{1,0:T(8,128)(2,1)S(1)}, u32[]{:S(2)}, u32[]{:S(2)}) collective-permute-start(bf16[256,512]{1,0:T(8,128)(2,1)S(1)} %get-tuple-element.38.refs_2_), channel_id=1, source_target_pairs={{0,8},{4,12},{8,16},{12,20},{16,24},{20,28},{1,9},{5,13},{9,17},{1... | collective-permute-start | bytes 786440 | tf_op jit(solution)/shard_map/ppermute | solution.py:402
  11.8 1.6 %collective-permute-start.1 = (f32[16,512]{1,0:T(8,128)S(1)}, f32[16,512]{1,0:T(8,128)S(1)}, u32[]{:S(2)}, u32[]{:S(2)}) collective-permute-start(f32[16,512]{1,0:T(8,128)S(1)} %add.7.mine), channel_id=1, source_target_pairs={{0,2},{1,3},{2,0},{3,1},{4,6},{5,7},{6,4},{7,5},{8,10},{9,11},{10,... | collective-permute-start | bytes 98312 | tf_op jit(solution)/shard_map/ppermute | solution.py:407
  13.4 1.6 %collective-permute-start.3 = (bf16[256,512]{1,0:T(8,128)(2,1)S(1)}, bf16[256,512]{1,0:T(8,128)(2,1)S(1)}, u32[]{:S(2)}, u32[]{:S(2)}) collective-permute-start(bf16[256,512]{1,0:T(8,128)(2,1)S(1)} %broadcast_select_fusion.3), channel_id=1, source_target_pairs={{0,4},{4,0},{8,12},{12,8},{16,20},{20,16},{24,28},{28,24},{1,5},{5... | collective-permute-start | bytes 786440 | tf_op jit(solution)/shard_map/ppermute | solution.py:407
  15.0 0.8 %collective-permute-done.1.theirs = f32[16,512]{1,0:T(8,128)S(1)} collective-permute-done((f32[16,512]{1,0:T(8,128)S(1)}, f32[16,512]{1,0:T(8,128)S(1)}, u32[]{:S(2)}, u32[]{:S(2)}) %collective-permute-start.1) | collective-permute-done | bytes 32800 | tf_op jit(solution)/shard_map/ppermute | solution.py:407
  15.8 0.3 adapt_values.1
  16.1 3.5 %collective-permute-start.6 = (bf16[512,256]{1,0:T(8,128)(2,1)S(1)}, bf16[512,256]{1,0:T(8,128)(2,1)S(1)}, u32[]{:S(2)}, u32[]{:S(2)}) collective-permute-start(bf16[512,256]{1,0:T(8,128)(2,1)S(1)} %get-tuple-element.47.refs_3_), channel_id=1, source_target_pairs={{0,8},{4,12},{8,16},{12,20},{16,24},{20,28},{1,9},{5,13},{9,17},{1... | collective-permute-start | bytes 786440 | tf_op jit(solution)/shard_map/ppermute | solution.py:402
  19.6 1.9 %collective-permute-start.7 = (bf16[512,256]{1,0:T(8,128)(2,1)S(1)}, bf16[512,256]{1,0:T(8,128)(2,1)S(1)}, u32[]{:S(2)}, u32[]{:S(2)}) collective-permute-start(bf16[512,256]{1,0:T(8,128)(2,1)S(1)} %get-tuple-element.46.refs_4_), channel_id=1, source_target_pairs={{0,8},{4,12},{8,16},{12,20},{16,24},{20,28},{1,9},{5,13},{9,17},{1... | collective-permute-start | bytes 786440 | tf_op jit(solution)/shard_map/ppermute | solution.py:402
  21.6 1.6 %collective-permute-start.5 = (bf16[256,512]{1,0:T(8,128)(2,1)S(1)}, bf16[256,512]{1,0:T(8,128)(2,1)S(1)}, u32[]{:S(2)}, u32[]{:S(2)}) collective-permute-start(bf16[256,512]{1,0:T(8,128)(2,1)S(1)} %broadcast_select_fusion.2), channel_id=1, source_target_pairs={{0,4},{4,0},{8,12},{12,8},{16,20},{20,16},{24,28},{28,24},{1,5},{5... | collective-permute-start | bytes 786440 | tf_op jit(solution)/shard_map/ppermute | solution.py:407
  23.2 2.2 %near_far.1 = (f32[1152,512]{1,0:T(8,128)S(1)}, bf16[8,512,512]{2,1,0:T(8,128)(2,1)S(1)}, f32[8,512]{1,0:T(8,128)S(1)}) custom-call(bf16[512,1024]{1,0:T(8,128)(2,1)S(1)} %copy-done, bf16[256,512]{1,0:T(8,128)(2,1)S(1)} %first_half.1.refs_1_, bf16[256,512]{1,0:T(8,128)(2,1)S(1)} %get-tuple-element.38.refs_2_, ...), custom_call_target="tpu_custom_call" | custom-call | tf_op jit(solution)/shard_map/near_far/pallas_call | solution.py:388
  25.4 0.9 %collective-permute-done.6.refs_6_ = bf16[512,256]{1,0:T(8,128)(2,1)S(1)} collective-permute-done((bf16[512,256]{1,0:T(8,128)(2,1)S(1)}, bf16[512,256]{1,0:T(8,128)(2,1)S(1)}, u32[]{:S(2)}, u32[]{:S(2)}) %collective-permute-start.6) | collective-permute-done | bytes 262176 | tf_op jit(solution)/shard_map/ppermute | solution.py:402
  26.4 1.6 %collective-permute-start.9 = (bf16[512,256]{1,0:T(8,128)(2,1)S(1)}, bf16[512,256]{1,0:T(8,128)(2,1)S(1)}, u32[]{:S(2)}, u32[]{:S(2)}) collective-permute-start(bf16[512,256]{1,0:T(8,128)(2,1)S(1)} %broadcast_select_fusion), channel_id=1, source_target_pairs={{0,4},{4,0},{8,12},{12,8},{16,20},{20,16},{24,28},{28,24},{1,5},{5... | collective-permute-start | bytes 786440 | tf_op jit(solution)/shard_map/ppermute | solution.py:407
  28.0 2.3 %collective-permute-done.7.refs_7_ = bf16[512,256]{1,0:T(8,128)(2,1)S(1)} collective-permute-done((bf16[512,256]{1,0:T(8,128)(2,1)S(1)}, bf16[512,256]{1,0:T(8,128)(2,1)S(1)}, u32[]{:S(2)}, u32[]{:S(2)}) %collective-permute-start.7) | collective-permute-done | bytes 262176 | tf_op jit(solution)/shard_map/ppermute | solution.py:402
  30.3 1.6 %collective-permute-start.8 = (bf16[512,256]{1,0:T(8,128)(2,1)S(1)}, bf16[512,256]{1,0:T(8,128)(2,1)S(1)}, u32[]{:S(2)}, u32[]{:S(2)}) collective-permute-start(bf16[512,256]{1,0:T(8,128)(2,1)S(1)} %broadcast_select_fusion.1), channel_id=1, source_target_pairs={{0,4},{4,0},{8,12},{12,8},{16,20},{20,16},{24,28},{28,24},{1,5},{5... | collective-permute-start | bytes 786440 | tf_op jit(solution)/shard_map/ppermute | solution.py:407
  31.9 1.1 %middle.1 = (f32[1152,512]{1,0:T(8,128)S(1)}, bf16[8,512,512]{2,1,0:T(8,128)(2,1)S(1)}, bf16[512,1024]{1,0:T(8,128)(2,1)}) custom-call(bf16[512,1024]{1,0:T(8,128)(2,1)S(1)} %copy-done, f32[1152,512]{1,0:T(8,128)S(1)} %get-tuple-element.40.refs_1_, bf16[8,512,512]{2,1,0:T(8,128)(2,1)S(1)} %get-tuple-element.41.refs_2_, ...), custom_call_target="tpu_custom_call" | custom-call | tf_op jit(solution)/shard_map/middle/pallas_call | solution.py:388
  33.0 3.5 %collective-permute-done.9.v = bf16[512,256]{1,0:T(8,128)(2,1)S(1)} collective-permute-done((bf16[512,256]{1,0:T(8,128)(2,1)S(1)}, bf16[512,256]{1,0:T(8,128)(2,1)S(1)}, u32[]{:S(2)}, u32[]{:S(2)}) %collective-permute-start.9) | collective-permute-done | bytes 262176 | tf_op jit(solution)/shard_map/ppermute | solution.py:407
  36.5 0.1 finish.2._
  36.6 3.6 %collective-permute-done.8.v = bf16[512,256]{1,0:T(8,128)(2,1)S(1)} collective-permute-done((bf16[512,256]{1,0:T(8,128)(2,1)S(1)}, bf16[512,256]{1,0:T(8,128)(2,1)S(1)}, u32[]{:S(2)}, u32[]{:S(2)}) %collective-permute-start.8) | collective-permute-done | bytes 262176 | tf_op jit(solution)/shard_map/ppermute | solution.py:407
  40.2 0.1 finish.3
  (12 shorter events, 0.1 us)
Async XLA Ops:
  1.0 12.4 %collective-permute-start.2 = (bf16[256,512]{1,0:T(8,128)(2,1)S(1)}, bf16[256,512]{1,0:T(8,128)(2,1)S(1)}, u32[]{:S(2)}, u32[]{:S(2)}) collective-permute-start(bf16[256,512]{1,0:T(8,128)(2,1)S(1)} %first_half.1.refs_1_), channel_id=1, source_target_pairs={{0,8},{4,12},{8,16},{12,20},{16,24},{20,28},{1,9},{5,13},{9,17},{1... | collective-permute-start | bytes 786440 | tf_op jit(solution)/shard_map/ppermute | solution.py:402
  5.9 9.9 %copy-start.1 = (bf16[512,512]{1,0:T(8,128)(2,1)S(1)}, bf16[512,512]{1,0:T(8,128)(2,1)}, u32[]{:S(2)}) copy-start(bf16[512,512]{1,0:T(8,128)(2,1)} %value.1) | copy-start | bytes 1572868
  5.9 17.3 %copy-start = (bf16[512,1024]{1,0:T(8,128)(2,1)S(1)}, bf16[512,1024]{1,0:T(8,128)(2,1)}, u32[]{:S(2)}) copy-start(bf16[512,1024]{1,0:T(8,128)(2,1)} %refs_0_.3) | copy-start | bytes 3145732
  8.2 3.6 %collective-permute-start = (f32[16,512]{1,0:T(8,128)S(1)}, f32[16,512]{1,0:T(8,128)S(1)}, u32[]{:S(2)}, u32[]{:S(2)}) collective-permute-start(f32[16,512]{1,0:T(8,128)S(1)} %get-tuple-element.28), channel_id=1, source_target_pairs={{0,1},{1,0},{2,3},{3,2},{4,5},{5,4},{6,7},{7,6},{8,9},{9,8},{10,11... | collective-permute-start | bytes 98312 | tf_op jit(solution)/shard_map/ppermute | solution.py:407
  8.3 13.3 %collective-permute-start.4 = (bf16[256,512]{1,0:T(8,128)(2,1)S(1)}, bf16[256,512]{1,0:T(8,128)(2,1)S(1)}, u32[]{:S(2)}, u32[]{:S(2)}) collective-permute-start(bf16[256,512]{1,0:T(8,128)(2,1)S(1)} %get-tuple-element.38.refs_2_), channel_id=1, source_target_pairs={{0,8},{4,12},{8,16},{12,20},{16,24},{20,28},{1,9},{5,13},{9,17},{1... | collective-permute-start | bytes 786440 | tf_op jit(solution)/shard_map/ppermute | solution.py:402
  11.8 4.0 %collective-permute-start.1 = (f32[16,512]{1,0:T(8,128)S(1)}, f32[16,512]{1,0:T(8,128)S(1)}, u32[]{:S(2)}, u32[]{:S(2)}) collective-permute-start(f32[16,512]{1,0:T(8,128)S(1)} %add.7.mine), channel_id=1, source_target_pairs={{0,2},{1,3},{2,0},{3,1},{4,6},{5,7},{6,4},{7,5},{8,10},{9,11},{10,... | collective-permute-start | bytes 98312 | tf_op jit(solution)/shard_map/ppermute | solution.py:407
  13.4 9.8 %collective-permute-start.3 = (bf16[256,512]{1,0:T(8,128)(2,1)S(1)}, bf16[256,512]{1,0:T(8,128)(2,1)S(1)}, u32[]{:S(2)}, u32[]{:S(2)}) collective-permute-start(bf16[256,512]{1,0:T(8,128)(2,1)S(1)} %broadcast_select_fusion.3), channel_id=1, source_target_pairs={{0,4},{4,0},{8,12},{12,8},{16,20},{20,16},{24,28},{28,24},{1,5},{5... | collective-permute-start | bytes 786440 | tf_op jit(solution)/shard_map/ppermute | solution.py:407
  16.1 10.2 %collective-permute-start.6 = (bf16[512,256]{1,0:T(8,128)(2,1)S(1)}, bf16[512,256]{1,0:T(8,128)(2,1)S(1)}, u32[]{:S(2)}, u32[]{:S(2)}) collective-permute-start(bf16[512,256]{1,0:T(8,128)(2,1)S(1)} %get-tuple-element.47.refs_3_), channel_id=1, source_target_pairs={{0,8},{4,12},{8,16},{12,20},{16,24},{20,28},{1,9},{5,13},{9,17},{1... | collective-permute-start | bytes 786440 | tf_op jit(solution)/shard_map/ppermute | solution.py:402
  19.6 10.7 %collective-permute-start.7 = (bf16[512,256]{1,0:T(8,128)(2,1)S(1)}, bf16[512,256]{1,0:T(8,128)(2,1)S(1)}, u32[]{:S(2)}, u32[]{:S(2)}) collective-permute-start(bf16[512,256]{1,0:T(8,128)(2,1)S(1)} %get-tuple-element.46.refs_4_), channel_id=1, source_target_pairs={{0,8},{4,12},{8,16},{12,20},{16,24},{20,28},{1,9},{5,13},{9,17},{1... | collective-permute-start | bytes 786440 | tf_op jit(solution)/shard_map/ppermute | solution.py:402
  21.6 10.3 %collective-permute-start.5 = (bf16[256,512]{1,0:T(8,128)(2,1)S(1)}, bf16[256,512]{1,0:T(8,128)(2,1)S(1)}, u32[]{:S(2)}, u32[]{:S(2)}) collective-permute-start(bf16[256,512]{1,0:T(8,128)(2,1)S(1)} %broadcast_select_fusion.2), channel_id=1, source_target_pairs={{0,4},{4,0},{8,12},{12,8},{16,20},{20,16},{24,28},{28,24},{1,5},{5... | collective-permute-start | bytes 786440 | tf_op jit(solution)/shard_map/ppermute | solution.py:407
  26.4 10.1 %collective-permute-start.9 = (bf16[512,256]{1,0:T(8,128)(2,1)S(1)}, bf16[512,256]{1,0:T(8,128)(2,1)S(1)}, u32[]{:S(2)}, u32[]{:S(2)}) collective-permute-start(bf16[512,256]{1,0:T(8,128)(2,1)S(1)} %broadcast_select_fusion), channel_id=1, source_target_pairs={{0,4},{4,0},{8,12},{12,8},{16,20},{20,16},{24,28},{28,24},{1,5},{5... | collective-permute-start | bytes 786440 | tf_op jit(solution)/shard_map/ppermute | solution.py:407
  30.3 9.9 %collective-permute-start.8 = (bf16[512,256]{1,0:T(8,128)(2,1)S(1)}, bf16[512,256]{1,0:T(8,128)(2,1)S(1)}, u32[]{:S(2)}, u32[]{:S(2)}) collective-permute-start(bf16[512,256]{1,0:T(8,128)(2,1)S(1)} %broadcast_select_fusion.1), channel_id=1, source_target_pairs={{0,4},{4,0},{8,12},{12,8},{16,20},{20,16},{24,28},{28,24},{1,5},{5... | collective-permute-start | bytes 786440 | tf_op jit(solution)/shard_map/ppermute | solution.py:407
